TPU v7x, 32 devices: a whole 2x2x4 slice. The times are simulated.
32 devices in a mesh: dp: 2 (over x), seq: 2 (over core), expert: 8 (over z, y).
Axes of the slice: x: 2, y: 2, z: 4, core: 2. Of those that a mesh axis runs over, the one named last changes fastest.
Arguments:
- out_grad: bfloat16 [4096, 2048], P(('dp', 'seq', 'expert')), may hold values from -6 to 6
- saved_act: bfloat16 [4096, 8, 768], P(('dp', 'seq', 'expert')), may hold values from -0.29882812 to 0.29882812
- gate_probs: float32 [4096, 8], P(('dp', 'seq', 'expert')), may hold values from 0.02 to 0.6
- routes: int32 [4096, 8], P(('dp', 'seq', 'expert')), may hold values from 0 to 15, all different within a row; in each aligned block of 128 rows (0 to 127, 128 to 255, ...) at most 72 rows name the same one
- w_down: bfloat16 [16, 768, 2048], P(('seq', 'expert'), 'dp'), may hold values from -0.21875 to 0.21875
Outputs:
- act_grad: bfloat16 [4096, 8, 768], P(('dp', 'seq', 'expert'))
- prob_grad: float32 [4096, 8], P(('dp', 'seq', 'expert'))
- weight_grad: bfloat16 [16, 768, 2048], P(('seq', 'expert'), 'dp')
Inputs may be any that keep to these rules, and one draw needn't show every extreme that they name: `routes`: within the rows of one device (aligned blocks of 128 tokens) no expert is named by more than 72 tokens, a bound that some block reaches; each token names 8 different experts.
All inputs are finite; a program needn't handle non-finite values.
Results may differ from a plain program's by a relative error of at most 0.014.
Values may be sent and summed in bfloat16 or wider, within the bound.
A program may use at most 128 MiB of HBM per device.

v0:
```python
import jax
import jax.numpy as jnp
from jax import lax
from jax.sharding import PartitionSpec as P


def local(out_grad, saved_act, gate_probs, routes, w_down):
    token_count = routes.shape[0]
    top_count = routes.shape[1]
    hidden_width = saved_act.shape[2]
    feature_width = out_grad.shape[1]
    owners = lax.axis_size(("seq", "expert"))
    pair_count = token_count * top_count
    most_rows = max(2, min(token_count, pair_count // owners + pair_count // (8 * owners)))
    capacity = owners * most_rows
    expert_of = routes.reshape(pair_count)
    one_hot = (expert_of[:, None] == jnp.arange(owners, dtype=jnp.int32)[None, :]).astype(jnp.int32)
    rank_of = jnp.sum((jnp.cumsum(one_hot, axis=0) - one_hot) * one_hot, axis=1)
    slot_of = expert_of * most_rows + rank_of
    source_row = (
        jnp.zeros((capacity,), jnp.int32).at[slot_of].set(jnp.arange(pair_count, dtype=jnp.int32))
    )
    prob_rows = jnp.zeros((capacity,), jnp.float32).at[slot_of].set(gate_probs.reshape(pair_count))
    grad_rows = jnp.take(out_grad, source_row // top_count, axis=0)
    act_rows = jnp.take(saved_act.reshape(pair_count, hidden_width), source_row, axis=0)
    send_grad = grad_rows.reshape(owners, most_rows * feature_width)
    send_act = act_rows.reshape(owners, most_rows * hidden_width)
    send_prob = prob_rows.reshape(owners, most_rows)
    arrived = (
        lax.all_to_all(send_grad, ("seq", "expert"), split_axis=0, concat_axis=0, tiled=True),
        lax.all_to_all(send_act, ("seq", "expert"), split_axis=0, concat_axis=0, tiled=True),
        lax.all_to_all(
            send_prob.astype(jnp.bfloat16),
            ("seq", "expert"),
            split_axis=0,
            concat_axis=0,
            tiled=True,
        ).astype(send_prob.dtype),
    )
    recv_grad = arrived[0].reshape(capacity, feature_width)
    recv_act = arrived[1].reshape(capacity, hidden_width)
    recv_prob = arrived[2].reshape(capacity)
    expert_grad = lax.dot_general(
        recv_grad,
        lax.all_gather(w_down, "dp", axis=1, tiled=True)[0],
        (((1,), (1,)), ((), ())),
        preferred_element_type=jnp.float32,
    )
    act_back = (recv_prob[:, None] * expert_grad).astype(jnp.bfloat16)
    prob_back = jnp.sum(recv_act.astype(jnp.float32) * expert_grad, axis=1)
    scaled = (recv_prob[:, None] * recv_grad.astype(jnp.float32)).astype(jnp.bfloat16)
    weight_part = lax.psum_scatter(
        lax.dot_general(
            recv_act, scaled, (((0,), (0,)), ((), ())), preferred_element_type=jnp.float32
        ).astype(jnp.bfloat16),
        "dp",
        scatter_dimension=0,
        tiled=True,
    )
    weight_grad = weight_part.reshape(w_down.shape)
    back_act = act_back.reshape(owners, most_rows * hidden_width)
    back_prob = prob_back.reshape(owners, most_rows)
    returned = (
        lax.all_to_all(back_act, ("seq", "expert"), split_axis=0, concat_axis=0, tiled=True),
        lax.all_to_all(
            back_prob.astype(jnp.bfloat16),
            ("seq", "expert"),
            split_axis=0,
            concat_axis=0,
            tiled=True,
        ).astype(back_prob.dtype),
    )
    slot_grad = returned[0].reshape(capacity, hidden_width)
    slot_prob = returned[1].reshape(capacity)
    act_grad = jnp.take(slot_grad, slot_of, axis=0).reshape(token_count, top_count, hidden_width)
    prob_grad = jnp.take(slot_prob, slot_of, axis=0).reshape(token_count, top_count)
    return (act_grad, prob_grad, weight_grad)


def solution(mesh):
    in_specs = (
        P(("dp", "seq", "expert"), None),
        P(("dp", "seq", "expert"), None, None),
        P(("dp", "seq", "expert"), None),
        P(("dp", "seq", "expert"), None),
        P(("seq", "expert"), "dp", None),
    )
    out_specs = (
        P(("dp", "seq", "expert"), None, None),
        P(("dp", "seq", "expert"), None),
        P(("seq", "expert"), "dp", None),
    )
    return jax.shard_map(local, mesh=mesh, in_specs=in_specs, out_specs=out_specs, check_vma=False)
```

profile of v0, /device:TPU:0, one launch (start us, length us, event | category | flops | bytes accessed | tf_op | source)
XLA Modules:
  0.0 490.4 jit_solution(15474529246030302256)
XLA Ops:
  19.3 7.4 %all-to-all-start = ((bf16[16,1,72]{2,1,0:T(2,128)(2,1)}), bf16[16,1,72]{2,1,0:T(2,128)(2,1)S(1)}, u32[]{:S(2)}, u32[]{:S(2)}) async-start(bf16[16,1,72]{2,1,0:T(2,128)(2,1)} %convert_element_type.104), calls=%async_computation | async-start | bytes 16384 | tf_op jit(solution)/shard_map/all_to_all | solution.py:32
  41.3 6.0 %gather_fusion = bf16[1152,2048]{1,0:T(8,128)(2,1)} fusion(bf16[128,2048]{1,0:T(8,128)(2,1)S(1)} %copy-done.2, s32[2048]{0:T(1024)S(1)} %pad_clamp_fusion.1), kind=kCustom, calls=%fused_computation | custom fusion | bytes 9441792 | tf_op jit(solution)/shard_map/jit(_take)/gather | solution.py:24
  66.3 6.2 %all-to-all-start.3 = ((bf16[16,2,27648]{2,1,0:T(2,128)(2,1)}), bf16[16,2,27648]{2,1,0:T(2,128)(2,1)S(1)}, u32[]{:S(2)}, u32[]{:S(2)}) async-start(bf16[16,2,27648]{2,1,0:T(2,128)(2,1)} %reshape.299), calls=%async_computation.3 | async-start | bytes 3538944 | tf_op jit(solution)/shard_map/all_to_all | solution.py:31
  77.3 6.8 %reduce.15 = bf16[16,147456]{1,0:T(8,128)(2,1)} reduce(bf16[16,1,147456]{2,0,1:T(8,128)(2,1)} %broadcast_select_fusion, bf16[]{:T(256)} %broadcast.127), dimensions={1}, to_apply=%copy.40.reduce_sub_computation | reduce | bytes 9437186 | tf_op jit(solution)/shard_map/jit(_take)/select_n | solution.py:24
  84.1 7.3 %reshape.295 = bf16[16,2,73728]{2,1,0:T(2,128)(2,1)} reshape(bf16[16,147456]{1,0:T(8,128)(2,1)} %reduce.15) | data formatting | bytes 9437184
  91.4 22.0 %all-to-all-done.3 = bf16[16,2,27648]{2,1,0:T(2,128)(2,1)S(1)} async-done(((bf16[16,2,27648]{2,1,0:T(2,128)(2,1)}), bf16[16,2,27648]{2,1,0:T(2,128)(2,1)S(1)}, u32[]{:S(2)}, u32[]{:S(2)}) %all-to-all-start.3) | async-done | bytes 1769504 | tf_op jit(solution)/shard_map/all_to_all | solution.py:31
  123.2 17.7 %mul.57 = f32[16,1,147456]{2,1,0:T(1,128)} reshape(f32[16,72,2048]{2,1,0:T(8,128)} %mul.56) | data formatting | bytes 18874368 | tf_op jit(solution)/shard_map/mul | solution.py:51
  140.9 6.3 %reshape.300 = bf16[16,1,55296]{2,1,0:T(2,128)(2,1)} reshape(bf16[16,2,27648]{2,1,0:T(2,128)(2,1)S(1)} %all-to-all-done.3) | data formatting | bytes 3538944
  147.2 39.0 %reduce.3 = bf16[16,55296]{1,0:T(8,128)(2,1)} reduce(bf16[16,1,55296]{2,1,0:T(2,128)(2,1)} %reshape.300, bf16[]{:T(256)} %constant.87), dimensions={1}, to_apply=%all_to_all.26.reduce_sub_computation | reduce | bytes 3538946 | tf_op jit(solution)/shard_map/all_to_all | solution.py:31
  188.3 30.1 %all-to-all-done.1 = bf16[16,2,73728]{2,1,0:T(2,128)(2,1)} async-done(((bf16[16,2,73728]{2,1,0:T(2,128)(2,1)}), bf16[16,2,73728]{2,1,0:T(2,128)(2,1)}, u32[]{:S(2)}, u32[]{:S(2)}) %all-to-all-start.1) | async-done | bytes 4718624 | tf_op jit(solution)/shard_map/all_to_all | solution.py:30
  218.4 12.8 %reshape.296 = bf16[16,1,147456]{2,1,0:T(2,128)(2,1)} reshape(bf16[16,2,73728]{2,1,0:T(2,128)(2,1)} %all-to-all-done.1) | data formatting | bytes 9437184
  231.3 62.7 %convert_reduce_fusion = (bf16[16,147456]{1,0:T(8,128)(2,1)}, bf16[16,147456]{1,0:T(8,128)(2,1)}) fusion(f32[16,1,147456]{2,1,0:T(1,128)} %mul.57, bf16[16,1,147456]{2,1,0:T(2,128)(2,1)} %reshape.296), kind=kLoop, calls=%fused_computation.6 | loop fusion | flops 7077888 | bytes 23592960 | tf_op jit(solution)/shard_map/convert_element_type | solution.py:51
  294.0 5.4 %convert_element_type.99 = bf16[1152,2048]{1,0:T(8,128)(2,1)} reshape(bf16[16,147456]{1,0:T(8,128)(2,1)} %get-tuple-element.12) | data formatting | bytes 9437184 | tf_op jit(solution)/shard_map/convert_element_type | solution.py:51
  299.4 8.1 %convolution_convert_fusion = bf16[768,2048]{1,0:T(8,128)(2,1)} fusion(bf16[1152,768]{1,0:T(8,128)(2,1)S(1)} %reshape.220, bf16[1152,2048]{1,0:T(8,128)(2,1)} %convert_element_type.99), kind=kOutput, calls=%fused_computation.9 | convolution fusion | flops 3625451520 | bytes 9633792 | tf_op jit(solution)/shard_map/dot_general | solution.py:53
  309.8 5.3 %reshape.217 = bf16[1152,2048]{1,0:T(8,128)(2,1)} reshape(bf16[16,147456]{1,0:T(8,128)(2,1)} %get-tuple-element.13) | data formatting | bytes 9437184 | tf_op jit(solution)/shard_map/reshape | solution.py:40
  315.1 9.8 %multiply_reduce_fusion = (bf16[1152]{0:T(1024)(128)(2,1)S(1)}, bf16[1152,768]{0,1:T(8,128)(2,1)}) fusion(bf16[1152,768]{0,1:T(8,128)(2,1)S(1)} %copy-done.4, f32[1152]{0:T(1024)S(1)} %reshape.222, bf16[1152,2048]{1,0:T(8,128)(2,1)} %reshape.217, bf16[1,768,2048]{2,1,0:T(8,128)(2,1)} %all-gather.2.cloned.1.call-done), kind=kOutput, calls=%fused_computation.7 | convolution fusion | flops 3628301312 | bytes 11410176 | tf_op jit(solution)/shard_map/dot_general | solution.py:43
  325.6 8.1 %all-to-all-start.4 = ((bf16[16,1,72]{2,1,0:T(2,128)(2,1)}), bf16[16,1,72]{2,1,0:T(2,128)(2,1)S(1)}, u32[]{:S(2)}, u32[]{:S(2)}) async-start(bf16[16,1,72]{2,1,0:T(2,128)(2,1)} %convert_element_type.105), calls=%async_computation.4 | async-start | bytes 16384 | tf_op jit(solution)/shard_map/all_to_all | solution.py:65
  340.0 38.5 %reduce.16 = bf16[16,55296]{1,0:T(8,128)(2,1)S(1)} reduce(bf16[16,1,55296]{2,1,0:T(2,128)(2,1)} %all_to_all.28, bf16[]{:T(256)} %broadcast.127), dimensions={1}, to_apply=%all_to_all.28.reduce_sub_computation | reduce | bytes 3538946 | tf_op jit(solution)/shard_map/all_to_all | solution.py:64
  380.8 6.3 %all-to-all-start.2 = ((bf16[16,2,27648]{2,1,0:T(2,128)(2,1)}), bf16[16,2,27648]{2,1,0:T(2,128)(2,1)S(1)}, u32[]{:S(2)}, u32[]{:S(2)}) async-start(bf16[16,2,27648]{2,1,0:T(2,128)(2,1)} %reshape.297), calls=%async_computation.2 | async-start | bytes 3538944 | tf_op jit(solution)/shard_map/all_to_all | solution.py:64
  387.3 6.2 %gather_fusion.3 = f32[1024]{0:T(1024)S(1)} fusion(f32[1152]{0:T(1024)S(1)} %reshape.223, s32[1024]{0:T(1024)S(1)} %broadcast_clamp_fusion), kind=kCustom, calls=%fused_computation.3 | custom fusion | bytes 12288 | tf_op jit(solution)/shard_map/jit(_take)/gather | solution.py:76
  394.3 33.8 %all-to-all-done.2 = bf16[16,2,27648]{2,1,0:T(2,128)(2,1)S(1)} async-done(((bf16[16,2,27648]{2,1,0:T(2,128)(2,1)}), bf16[16,2,27648]{2,1,0:T(2,128)(2,1)S(1)}, u32[]{:S(2)}, u32[]{:S(2)}) %all-to-all-start.2) | async-done | bytes 1769504 | tf_op jit(solution)/shard_map/all_to_all | solution.py:64
  428.1 6.2 %reshape.298 = bf16[16,1,55296]{2,1,0:T(2,128)(2,1)} reshape(bf16[16,2,27648]{2,1,0:T(2,128)(2,1)S(1)} %all-to-all-done.2) | data formatting | bytes 3538944
  434.3 39.0 %reduce.2 = bf16[16,55296]{1,0:T(8,128)(2,1)} reduce(bf16[16,1,55296]{2,1,0:T(2,128)(2,1)} %reshape.298, bf16[]{:T(256)} %constant.87), dimensions={1}, to_apply=%all_to_all.25.reduce_sub_computation | reduce | bytes 3538946 | tf_op jit(solution)/shard_map/all_to_all | solution.py:64
  475.4 5.2 %gather_fusion.1 = bf16[1024,768]{1,0:T(8,128)(2,1)} fusion(bf16[1152,768]{1,0:T(8,128)(2,1)S(1)} %reshape.218, s32[1024]{0:T(1024)S(1)} %broadcast_clamp_fusion), kind=kCustom, calls=%fused_computation.1 | custom fusion | bytes 3149824 | tf_op jit(solution)/shard_map/jit(_take)/gather | solution.py:75
  (78 shorter events, 79.5 us)
Async XLA Ops:
  7.2 26.0 %copy-start = (bf16[128,8,768]{2,1,0:T(8,128)(2,1)S(1)}, bf16[128,8,768]{2,1,0:T(8,128)(2,1)}, u32[]{:S(2)}) copy-start(bf16[128,8,768]{2,1,0:T(8,128)(2,1)} %param.6) | copy-start | bytes 4718596
  19.3 47.0 %all-to-all-start = ((bf16[16,1,72]{2,1,0:T(2,128)(2,1)}), bf16[16,1,72]{2,1,0:T(2,128)(2,1)S(1)}, u32[]{:S(2)}, u32[]{:S(2)}) async-start(bf16[16,1,72]{2,1,0:T(2,128)(2,1)} %convert_element_type.104), calls=%async_computation | async-start | bytes 16384 | tf_op jit(solution)/shard_map/all_to_all | solution.py:32
  37.8 1.8 copy-start.3
  37.8 3.5 copy-start.2
  66.3 47.2 %all-to-all-start.3 = ((bf16[16,2,27648]{2,1,0:T(2,128)(2,1)}), bf16[16,2,27648]{2,1,0:T(2,128)(2,1)S(1)}, u32[]{:S(2)}, u32[]{:S(2)}) async-start(bf16[16,2,27648]{2,1,0:T(2,128)(2,1)} %reshape.299), calls=%async_computation.3 | async-start | bytes 3538944 | tf_op jit(solution)/shard_map/all_to_all | solution.py:31
  113.4 105.0 %all-to-all-start.1 = ((bf16[16,2,73728]{2,1,0:T(2,128)(2,1)}), bf16[16,2,73728]{2,1,0:T(2,128)(2,1)}, u32[]{:S(2)}, u32[]{:S(2)}) async-start(bf16[16,2,73728]{2,1,0:T(2,128)(2,1)} %reshape.295), calls=%async_computation.1 | async-start | bytes 9437184 | tf_op jit(solution)/shard_map/all_to_all | solution.py:30
  118.1 197.1 %all-gather.2.cloned.1.call-start = ((), (), s32[]{:S(2)}) async-start(), calls=%async_computation.6 | async-start | bytes 4718592 | tf_op jit(solution)/shard_map/all_gather | solution.py:45
  118.8 364.6 %reduce-scatter.2.cloned.1.call-start = ((), (), s32[]{:S(2)}) async-start(), calls=%async_computation.7 | async-start | bytes 4718592 | tf_op jit(solution)/shard_map/reduce_scatter | solution.py:52
  309.8 5.3 %copy-start.4 = (bf16[1152,768]{0,1:T(8,128)(2,1)S(1)}, bf16[1152,768]{0,1:T(8,128)(2,1)}, u32[]{:S(2)}) copy-start(bf16[1152,768]{0,1:T(8,128)(2,1)} %copy.44) | copy-start | bytes 5308420
  325.6 55.2 %all-to-all-start.4 = ((bf16[16,1,72]{2,1,0:T(2,128)(2,1)}), bf16[16,1,72]{2,1,0:T(2,128)(2,1)S(1)}, u32[]{:S(2)}, u32[]{:S(2)}) async-start(bf16[16,1,72]{2,1,0:T(2,128)(2,1)} %convert_element_type.105), calls=%async_computation.4 | async-start | bytes 16384 | tf_op jit(solution)/shard_map/all_to_all | solution.py:65
  380.8 47.3 %all-to-all-start.2 = ((bf16[16,2,27648]{2,1,0:T(2,128)(2,1)}), bf16[16,2,27648]{2,1,0:T(2,128)(2,1)S(1)}, u32[]{:S(2)}, u32[]{:S(2)}) async-start(bf16[16,2,27648]{2,1,0:T(2,128)(2,1)} %reshape.297), calls=%async_computation.2 | async-start | bytes 3538944 | tf_op jit(solution)/shard_map/all_to_all | solution.py:64
  475.4 8.0 %copy-start.1 = (bf16[128,8,768]{2,1,0:T(8,128)(2,1)S(1)}, bf16[128,8,768]{2,1,0:T(8,128)(2,1)}, u32[]{:S(2)}) copy-start(bf16[128,8,768]{2,1,0:T(8,128)(2,1)} %param.6) | copy-start | bytes 4718596
Sparse Core Ops, SparseCore 0:
  120.5 46.1 all-gather.1
  307.6 47.1 reduce-scatter.1
where the time goes:
time: 500 us; the launch traced here: 490 us
  other arithmetic  203 us (41%)
  local copies, waits for them, and re-layouts  136 us (27%)
  waiting for transfers between devices  86.7 us (17%)
  starting transfers between devices  32.6 us (7%)
  matrix products  17.9 us (4%)
  between operations  14.6 us (3%)
    all_to_all x2, other arithmetic, local(): lax.all_to_all(back_act, ('seq', 'expert'), split_axis=0, concat_axis=0,...  77.5 us
    convert_element_type x1, other arithmetic, local(): (recv_prob[:, None] * recv_grad.astype(jnp.float32)).astype(jnp.bfloat16)  62.7 us
    unnamed x19, local copies, waits for them, and re-layouts  41.1 us
    all_to_all x1, other arithmetic, local(): lax.all_to_all(send_act, ('seq', 'expert'), split_axis=0, concat_axis=0,...  39 us
    all_to_all x1, waiting for transfers between devices, local(): lax.all_to_all(back_act, ('seq', 'expert'), split_axis=0, concat_axis=0,...  33.8 us
    all_to_all x1, waiting for transfers between devices, local(): lax.all_to_all(send_grad, ('seq', 'expert'), split_axis=0, concat_axis=0,...  30.1 us
    mul x2, local copies, waits for them, and re-layouts, local(): recv_prob[:, None] * recv_grad.astype(jnp.float32)  22 us
    all_to_all x1, waiting for transfers between devices, local(): lax.all_to_all(send_act, ('seq', 'expert'), split_axis=0, concat_axis=0,...  22 us
  transfers between devices with their start and end apart: 7, of which 3 were waited for; matrix products, arithmetic and copies ran while one was open for 70% of the time, Pallas kernels for 0%

commit v1 on v0

--- a/solution.py
+++ b/solution.py
@@ -1,7 +1,46 @@
+import functools
 import jax
 import jax.numpy as jnp
 from jax import lax
 from jax.sharding import PartitionSpec as P
+
+
+def place_counts(field_in, at_axis, xs):
+    current_value = field_in.shape
+    s_next = field_in.reshape(
+        *current_value[:at_axis], xs, current_value[at_axis] // xs, *current_value[at_axis + 1 :]
+    )
+    res = jnp.moveaxis(s_next, at_axis, 0)
+    return res
+
+
+def build_the_sector(t0, which_dim):
+    t0 = jnp.moveaxis(t0, 0, which_dim)
+    parts_out = t0.shape
+    val2 = t0.reshape(
+        *parts_out[:which_dim],
+        parts_out[which_dim] * parts_out[which_dim + 1],
+        *parts_out[which_dim + 2 :]
+    )
+    return val2
+
+
+def follow_table(point, ax_name, xx, local_array):
+    seen_now = lax.axis_index(ax_name)
+    found_now = lax.axis_size(ax_name)
+    near, high = (found_now, seen_now)
+    long_array = place_counts(point, xx, near)
+    newest = long_array
+    for w in range(1, near):
+        work_now, raw_out = ((high + w) % near, (high - w) % near)
+        z2 = lax.dynamic_index_in_dim(long_array, work_now, 0)
+        e_next = lax.ppermute(z2, ax_name, [(dev_i, (dev_i + w) % near) for dev_i in range(near)])
+        newest = lax.dynamic_update_slice_in_dim(newest, e_next, raw_out, axis=0)
+    answer = build_the_sector(newest, local_array)
+    return answer
+
+
+store_the_patches = functools.partial(follow_table, ax_name=("seq", "expert"), xx=0, local_array=0)
 
 
 def local(out_grad, saved_act, gate_probs, routes, w_down):
@@ -28,7 +67,7 @@
     send_prob = prob_rows.reshape(owners, most_rows)
     arrived = (
         lax.all_to_all(send_grad, ("seq", "expert"), split_axis=0, concat_axis=0, tiled=True),
-        lax.all_to_all(send_act, ("seq", "expert"), split_axis=0, concat_axis=0, tiled=True),
+        store_the_patches(send_act),
         lax.all_to_all(
             send_prob.astype(jnp.bfloat16),
             ("seq", "expert"),

time: 500 us -> 619 us (1.24)
  local copies, waits for them, and re-layouts: 136 us -> 196 us
  waiting for transfers between devices: 86.7 us -> 145 us
  starting transfers between devices: 32.6 us -> 80.3 us
  other arithmetic: 203 us -> 160 us
    ppermute x0 -> x15, waiting for transfers between devices: none -> 112 us  [follow_table(): lax.ppermute(z2, ax_name, [(dev_i, (dev_i + w) % near) for dev_i in range...]
    dynamic_update_slice x0 -> x15, local copies, waits for them, and re-layouts: none -> 69.9 us  [follow_table(): newest = lax.dynamic_update_slice_in_dim(newest, e_next, raw_out, axis=0)]
    all_to_all x1 -> x0, other arithmetic: 39 us -> none  [local(): lax.all_to_all(send_act, ('seq', 'expert'), split_axis=0, concat_axis=0,...]
    ppermute x0 -> x15, starting transfers between devices: none -> 37.3 us  [follow_table(): lax.ppermute(z2, ax_name, [(dev_i, (dev_i + w) % near) for dev_i in range...]
    all_to_all x1, waiting for transfers between devices: 30.1 us -> 0.01 us  [local(): lax.all_to_all(send_grad, ('seq', 'expert'), split_axis=0, concat_axis=0,...]
    all_to_all x1 -> x0, waiting for transfers between devices: 22 us -> none  [local(): lax.all_to_all(send_act, ('seq', 'expert'), split_axis=0, concat_axis=0,...]
    all_to_all x1, starting transfers between devices: 8.08 us -> 22.4 us  [local(): lax.all_to_all(back_prob.astype(jnp.bfloat16), ('seq', 'expert'), split_a...]
    unnamed x19 -> x25, local copies, waits for them, and re-layouts: 41.1 us -> 31.8 us
  transfers between devices with their start and end apart: 7 -> 21, of which waited for: 3 -> 4; matrix products, arithmetic and copies ran while one was open for 70% -> 58% of each run, Pallas kernels for 0% -> 0%
where the time goes in v1:
time: 619 us; the launch traced here: 613 us
  local copies, waits for them, and re-layouts  196 us (32%)
  other arithmetic  160 us (26%)
  waiting for transfers between devices  145 us (23%)
  starting transfers between devices  80.3 us (13%)
  matrix products  15.6 us (3%)
  between operations  15.4 us (2%)
    ppermute x15, waiting for transfers between devices, follow_table(): lax.ppermute(z2, ax_name, [(dev_i, (dev_i + w) % near) for dev_i in range...  112 us
    all_to_all x2, other arithmetic, local(): lax.all_to_all(back_act, ('seq', 'expert'), split_axis=0, concat_axis=0,...  76.3 us
    dynamic_update_slice x15, local copies, waits for them, and re-layouts, follow_table(): newest = lax.dynamic_update_slice_in_dim(newest, e_next, raw_out, axis=0)  69.9 us
    convert_element_type x1, other arithmetic, local(): (recv_prob[:, None] * recv_grad.astype(jnp.float32)).astype(jnp.bfloat16)  62.9 us
    ppermute x15, starting transfers between devices, follow_table(): lax.ppermute(z2, ax_name, [(dev_i, (dev_i + w) % near) for dev_i in range...  37.3 us
    all_to_all x1, waiting for transfers between devices, local(): lax.all_to_all(back_act, ('seq', 'expert'), split_axis=0, concat_axis=0,...  33.3 us
    unnamed x25, local copies, waits for them, and re-layouts  31.8 us
    all_to_all x1, starting transfers between devices, local(): lax.all_to_all(back_prob.astype(jnp.bfloat16), ('seq', 'expert'), split_a...  22.4 us
  transfers between devices with their start and end apart: 21, of which 4 were waited for; matrix products, arithmetic and copies ran while one was open for 58% of the time, Pallas kernels for 0%

profile of v1, /device:TPU:0, one launch (start us, length us, event | category | flops | bytes accessed | tf_op | source)
XLA Modules:
  0.0 612.7 jit_solution(5694775047393730923)
XLA Ops:
  19.3 7.4 %all-to-all-start = ((bf16[16,1,72]{2,1,0:T(2,128)(2,1)}), bf16[16,1,72]{2,1,0:T(2,128)(2,1)S(1)}, u32[]{:S(2)}, u32[]{:S(2)}) async-start(bf16[16,1,72]{2,1,0:T(2,128)(2,1)} %convert_element_type.104), calls=%async_computation | async-start | bytes 16384 | tf_op jit(solution)/shard_map/all_to_all | solution.py:71
  38.3 5.9 gather_fusion
  44.2 5.3 gather.25
  55.0 6.7 %reduce.13 = bf16[16,147456]{1,0:T(8,128)(2,1)} reduce(bf16[16,1,147456]{2,0,1:T(8,128)(2,1)} %broadcast_select_fusion, bf16[]{:T(256)} %broadcast.163), dimensions={1}, to_apply=%copy.39.reduce_sub_computation | reduce | bytes 9437186 | tf_op jit(solution)/shard_map/jit(_take)/select_n | solution.py:63
  61.7 7.3 %reshape.289 = bf16[16,2,73728]{2,1,0:T(2,128)(2,1)} reshape(bf16[16,147456]{1,0:T(8,128)(2,1)} %reduce.13) | data formatting | bytes 9437184
  77.5 6.2 %all-to-all-start.1 = ((bf16[16,2,73728]{2,1,0:T(2,128)(2,1)}), bf16[16,2,73728]{2,1,0:T(2,128)(2,1)}, u32[]{:S(2)}, u32[]{:S(2)}) async-start(bf16[16,2,73728]{2,1,0:T(2,128)(2,1)} %reshape.289), calls=%async_computation.1 | async-start | bytes 9437184 | tf_op jit(solution)/shard_map/all_to_all | solution.py:69
  98.5 71.4 %collective-permute-done = bf16[1,1,55296]{2,0,1:T(2,128)(2,1)S(1)} collective-permute-done((bf16[1,1,55296]{2,0,1:T(2,128)(2,1)S(1)}, bf16[1,1,55296]{2,0,1:T(2,128)(2,1)S(1)}, u32[]{:S(2)}, u32[]{:S(2)}) %collective-permute-start) | collective-permute-done | bytes 110624 | tf_op jit(solution)/shard_map/ppermute | solution.py:37
  175.1 38.0 %collective-permute-done.2 = bf16[1,1,55296]{2,0,1:T(2,128)(2,1)S(1)} collective-permute-done((bf16[1,1,55296]{2,0,1:T(2,128)(2,1)S(1)}, bf16[1,1,55296]{2,0,1:T(2,128)(2,1)S(1)}, u32[]{:S(2)}, u32[]{:S(2)}) %collective-permute-start.2) | collective-permute-done | bytes 110624 | tf_op jit(solution)/shard_map/ppermute | solution.py:37
  213.9 5.2 collective-permute-start.8
  219.1 8.3 %collective-permute-start.9 = (bf16[1,1,55296]{2,0,1:T(2,128)(2,1)S(1)}, bf16[1,1,55296]{2,0,1:T(2,128)(2,1)}, u32[]{:S(2)}, u32[]{:S(2)}) collective-permute-start(bf16[1,1,55296]{2,0,1:T(2,128)(2,1)S(1)} %get-tuple-element.25), channel_id=1, source_target_pairs={{0,10},{1,11},{2,12},{3,13},{4,14},{5,15},{6,0},{7,1},{8,2},{9,3},... | collective-permute-start | bytes 331784 | tf_op jit(solution)/shard_map/ppermute | solution.py:37
  244.0 17.5 %mul.61 = f32[16,1,147456]{2,1,0:T(1,128)} reshape(f32[16,72,2048]{2,1,0:T(8,128)} %mul.60) | data formatting | bytes 18874368 | tf_op jit(solution)/shard_map/mul | solution.py:90
  332.5 12.8 %reshape.290 = bf16[16,1,147456]{2,1,0:T(2,128)(2,1)} reshape(bf16[16,2,73728]{2,1,0:T(2,128)(2,1)} %all-to-all-done.1) | data formatting | bytes 9437184
  345.3 62.9 %convert_reduce_fusion = (bf16[16,147456]{1,0:T(8,128)(2,1)}, bf16[16,147456]{1,0:T(8,128)(2,1)}) fusion(f32[16,1,147456]{2,1,0:T(1,128)} %mul.61, bf16[16,1,147456]{2,1,0:T(2,128)(2,1)} %reshape.290), kind=kLoop, calls=%fused_computation.6 | loop fusion | flops 7077888 | bytes 23592960 | tf_op jit(solution)/shard_map/convert_element_type | solution.py:90
  413.4 8.1 %convolution_convert_fusion = bf16[768,2048]{1,0:T(8,128)(2,1)} fusion(bf16[1152,768]{1,0:T(8,128)(2,1)S(1)} %reshape_reshape.4, bf16[1152,2048]{1,0:T(8,128)(2,1)} %convert_element_type.99), kind=kOutput, calls=%fused_computation.9 | convolution fusion | flops 3625451520 | bytes 9633792 | tf_op jit(solution)/shard_map/dot_general | solution.py:92
  422.6 5.2 reshape.213
  427.9 7.6 %fusion = f32[1152,768]{0,1:T(8,128)S(1)} fusion(bf16[1152,2048]{1,0:T(8,128)(2,1)} %reshape.213, bf16[1,768,2048]{2,1,0:T(8,128)(2,1)} %all-gather.2.cloned.1.call-done), kind=kOutput, calls=%fused_computation.10 | convolution fusion | flops 3623878656 | bytes 11403264 | tf_op jit(solution)/shard_map/dot_general | solution.py:82
  436.8 22.4 %all-to-all-start.3 = ((bf16[16,1,72]{2,1,0:T(2,128)(2,1)}), bf16[16,1,72]{2,1,0:T(2,128)(2,1)S(1)}, u32[]{:S(2)}, u32[]{:S(2)}) async-start(bf16[16,1,72]{2,1,0:T(2,128)(2,1)} %convert_element_type.105), calls=%async_computation.3 | async-start | bytes 16384 | tf_op jit(solution)/shard_map/all_to_all | solution.py:104
  463.8 38.5 %reduce.14 = bf16[16,55296]{1,0:T(8,128)(2,1)S(1)} reduce(bf16[16,1,55296]{2,1,0:T(2,128)(2,1)} %all_to_all.23, bf16[]{:T(256)} %broadcast.163), dimensions={1}, to_apply=%all_to_all.23.reduce_sub_computation | reduce | bytes 3538946 | tf_op jit(solution)/shard_map/all_to_all | solution.py:103
  504.7 6.5 %all-to-all-start.2 = ((bf16[16,2,27648]{2,1,0:T(2,128)(2,1)}), bf16[16,2,27648]{2,1,0:T(2,128)(2,1)S(1)}, u32[]{:S(2)}, u32[]{:S(2)}) async-start(bf16[16,2,27648]{2,1,0:T(2,128)(2,1)} %reshape.291), calls=%async_computation.2 | async-start | bytes 3538944 | tf_op jit(solution)/shard_map/all_to_all | solution.py:103
  511.9 6.1 %gather_fusion.3 = f32[1024]{0:T(1024)S(1)} fusion(f32[1152]{0:T(1024)S(1)} %reshape.218, s32[1024]{0:T(1024)S(1)} %broadcast_clamp_fusion), kind=kCustom, calls=%fused_computation.3 | custom fusion | bytes 12288 | tf_op jit(solution)/shard_map/jit(_take)/gather | solution.py:115
  518.9 33.3 %all-to-all-done.2 = bf16[16,2,27648]{2,1,0:T(2,128)(2,1)S(1)} async-done(((bf16[16,2,27648]{2,1,0:T(2,128)(2,1)}), bf16[16,2,27648]{2,1,0:T(2,128)(2,1)S(1)}, u32[]{:S(2)}, u32[]{:S(2)}) %all-to-all-start.2) | async-done | bytes 1769504 | tf_op jit(solution)/shard_map/all_to_all | solution.py:103
  552.2 6.3 %reshape.292 = bf16[16,1,55296]{2,1,0:T(2,128)(2,1)} reshape(bf16[16,2,27648]{2,1,0:T(2,128)(2,1)S(1)} %all-to-all-done.2) | data formatting | bytes 3538944
  558.5 37.8 %reduce.2 = bf16[16,55296]{1,0:T(8,128)(2,1)S(1)} reduce(bf16[16,1,55296]{2,1,0:T(2,128)(2,1)} %reshape.292, bf16[]{:T(256)} %constant.310), dimensions={1}, to_apply=%all_to_all.21.reduce_sub_computation | reduce | bytes 3538946 | tf_op jit(solution)/shard_map/all_to_all | solution.py:103
  597.2 5.6 gather_fusion.1
  (127 shorter events, 164.9 us)
Async XLA Ops:
  7.2 64.0 %copy-start = (bf16[128,8,768]{2,1,0:T(8,128)(2,1)S(1)}, bf16[128,8,768]{2,1,0:T(8,128)(2,1)}, u32[]{:S(2)}) copy-start(bf16[128,8,768]{2,1,0:T(8,128)(2,1)} %param.6) | copy-start | bytes 4718596
  8.1 25.4 %copy-start.4 = (s32[128,8]{1,0:T(8,128)}, s32[128,8]{1,0:T(8,128)S(1)}, u32[]{:S(2)}) copy-start(s32[128,8]{1,0:T(8,128)S(1)} %copy.32) | copy-start | bytes 12292
  14.3 17.1 %copy-start.7 = (s32[1024,1]{0,1:T(1,128)}, s32[1024,1]{0,1:T(1,128)S(1)}, u32[]{:S(2)}) copy-start(s32[1024,1]{0,1:T(1,128)S(1)} %compare_select_fusion.1) | copy-start | bytes 12292
  19.3 58.2 %all-to-all-start = ((bf16[16,1,72]{2,1,0:T(2,128)(2,1)}), bf16[16,1,72]{2,1,0:T(2,128)(2,1)S(1)}, u32[]{:S(2)}, u32[]{:S(2)}) async-start(bf16[16,1,72]{2,1,0:T(2,128)(2,1)} %convert_element_type.104), calls=%async_computation | async-start | bytes 16384 | tf_op jit(solution)/shard_map/all_to_all | solution.py:71
  77.5 254.9 %all-to-all-start.1 = ((bf16[16,2,73728]{2,1,0:T(2,128)(2,1)}), bf16[16,2,73728]{2,1,0:T(2,128)(2,1)}, u32[]{:S(2)}, u32[]{:S(2)}) async-start(bf16[16,2,73728]{2,1,0:T(2,128)(2,1)} %reshape.289), calls=%async_computation.1 | async-start | bytes 9437184 | tf_op jit(solution)/shard_map/all_to_all | solution.py:69
  83.7 344.2 %all-gather.2.cloned.1.call-start = ((), (), s32[]{:S(2)}) async-start(), calls=%async_computation.5 | async-start | bytes 4718592 | tf_op jit(solution)/shard_map/all_gather | solution.py:84
  90.0 79.9 %collective-permute-start = (bf16[1,1,55296]{2,0,1:T(2,128)(2,1)S(1)}, bf16[1,1,55296]{2,0,1:T(2,128)(2,1)S(1)}, u32[]{:S(2)}, u32[]{:S(2)}) collective-permute-start(bf16[1,1,55296]{2,0,1:T(2,128)(2,1)S(1)} %get-tuple-element.34), channel_id=1, source_target_pairs={{0,1},{1,2},{2,3},{3,4},{4,5},{5,6},{6,7},{7,8},{8,9},{9,10},{10,1... | collective-permute-start | bytes 331784 | tf_op jit(solution)/shard_map/ppermute | solution.py:37
  91.9 78.0 %collective-permute-start.1 = (bf16[1,1,55296]{2,0,1:T(2,128)(2,1)S(1)}, bf16[1,1,55296]{2,0,1:T(2,128)(2,1)S(1)}, u32[]{:S(2)}, u32[]{:S(2)}) collective-permute-start(bf16[1,1,55296]{2,0,1:T(2,128)(2,1)S(1)} %get-tuple-element.33), channel_id=1, source_target_pairs={{0,2},{1,3},{2,4},{3,5},{4,6},{5,7},{6,8},{7,9},{8,10},{9,11},{10,... | collective-permute-start | bytes 331784 | tf_op jit(solution)/shard_map/ppermute | solution.py:37
  93.4 119.7 %collective-permute-start.2 = (bf16[1,1,55296]{2,0,1:T(2,128)(2,1)S(1)}, bf16[1,1,55296]{2,0,1:T(2,128)(2,1)S(1)}, u32[]{:S(2)}, u32[]{:S(2)}) collective-permute-start(bf16[1,1,55296]{2,0,1:T(2,128)(2,1)S(1)} %get-tuple-element.32), channel_id=1, source_target_pairs={{0,3},{1,4},{2,5},{3,6},{4,7},{5,8},{6,9},{7,10},{8,11},{9,12},{10... | collective-permute-start | bytes 331784 | tf_op jit(solution)/shard_map/ppermute | solution.py:37
  95.7 118.1 %collective-permute-start.3 = (bf16[1,1,55296]{2,0,1:T(2,128)(2,1)S(1)}, bf16[1,1,55296]{2,0,1:T(2,128)(2,1)S(1)}, u32[]{:S(2)}, u32[]{:S(2)}) collective-permute-start(bf16[1,1,55296]{2,0,1:T(2,128)(2,1)S(1)} %get-tuple-element.31), channel_id=1, source_target_pairs={{0,4},{1,5},{2,6},{3,7},{4,8},{5,9},{6,10},{7,11},{8,12},{9,13},{1... | collective-permute-start | bytes 331784 | tf_op jit(solution)/shard_map/ppermute | solution.py:37
  96.7 122.4 %collective-permute-start.4 = (bf16[1,1,55296]{2,0,1:T(2,128)(2,1)S(1)}, bf16[1,1,55296]{2,0,1:T(2,128)(2,1)S(1)}, u32[]{:S(2)}, u32[]{:S(2)}) collective-permute-start(bf16[1,1,55296]{2,0,1:T(2,128)(2,1)S(1)} %get-tuple-element.30), channel_id=1, source_target_pairs={{0,5},{1,6},{2,7},{3,8},{4,9},{5,10},{6,11},{7,12},{8,13},{9,14},{... | collective-permute-start | bytes 331784 | tf_op jit(solution)/shard_map/ppermute | solution.py:37
  169.9 57.5 %collective-permute-start.5 = (bf16[1,1,55296]{2,0,1:T(2,128)(2,1)S(1)}, bf16[1,1,55296]{2,0,1:T(2,128)(2,1)S(1)}, u32[]{:S(2)}, u32[]{:S(2)}) collective-permute-start(bf16[1,1,55296]{2,0,1:T(2,128)(2,1)S(1)} %get-tuple-element.29), channel_id=1, source_target_pairs={{0,6},{1,7},{2,8},{3,9},{4,10},{5,11},{6,12},{7,13},{8,14},{9,15},... | collective-permute-start | bytes 331784 | tf_op jit(solution)/shard_map/ppermute | solution.py:37
  169.9 57.9 %collective-permute-start.6 = (bf16[1,1,55296]{2,0,1:T(2,128)(2,1)S(1)}, bf16[1,1,55296]{2,0,1:T(2,128)(2,1)S(1)}, u32[]{:S(2)}, u32[]{:S(2)}) collective-permute-start(bf16[1,1,55296]{2,0,1:T(2,128)(2,1)S(1)} %get-tuple-element.28), channel_id=1, source_target_pairs={{0,7},{1,8},{2,9},{3,10},{4,11},{5,12},{6,13},{7,14},{8,15},{9,0},... | collective-permute-start | bytes 331784 | tf_op jit(solution)/shard_map/ppermute | solution.py:37
  213.1 17.4 %collective-permute-start.7 = (bf16[1,1,55296]{2,0,1:T(2,128)(2,1)S(1)}, bf16[1,1,55296]{2,0,1:T(2,128)(2,1)S(1)}, u32[]{:S(2)}, u32[]{:S(2)}) collective-permute-start(bf16[1,1,55296]{2,0,1:T(2,128)(2,1)S(1)} %get-tuple-element.27), channel_id=1, source_target_pairs={{0,8},{1,9},{2,10},{3,11},{4,12},{5,13},{6,14},{7,15},{8,0},{9,1},... | collective-permute-start | bytes 331784 | tf_op jit(solution)/shard_map/ppermute | solution.py:37
  213.9 22.7 %collective-permute-start.8 = (bf16[1,1,55296]{2,0,1:T(2,128)(2,1)S(1)}, bf16[1,1,55296]{2,0,1:T(2,128)(2,1)}, u32[]{:S(2)}, u32[]{:S(2)}) collective-permute-start(bf16[1,1,55296]{2,0,1:T(2,128)(2,1)S(1)} %get-tuple-element.26), channel_id=1, source_target_pairs={{0,9},{1,10},{2,11},{3,12},{4,13},{5,14},{6,15},{7,0},{8,1},{9,2},... | collective-permute-start | bytes 331784 | tf_op jit(solution)/shard_map/ppermute | solution.py:37
  219.1 17.5 %collective-permute-start.9 = (bf16[1,1,55296]{2,0,1:T(2,128)(2,1)S(1)}, bf16[1,1,55296]{2,0,1:T(2,128)(2,1)}, u32[]{:S(2)}, u32[]{:S(2)}) collective-permute-start(bf16[1,1,55296]{2,0,1:T(2,128)(2,1)S(1)} %get-tuple-element.25), channel_id=1, source_target_pairs={{0,10},{1,11},{2,12},{3,13},{4,14},{5,15},{6,0},{7,1},{8,2},{9,3},... | collective-permute-start | bytes 331784 | tf_op jit(solution)/shard_map/ppermute | solution.py:37
  227.4 78.5 %collective-permute-start.10 = (bf16[1,1,55296]{2,0,1:T(2,128)(2,1)}, bf16[1,1,55296]{2,0,1:T(2,128)(2,1)}, u32[]{:S(2)}, u32[]{:S(2)}) collective-permute-start(bf16[1,1,55296]{2,0,1:T(2,128)(2,1)} %get-tuple-element.24), channel_id=1, source_target_pairs={{0,11},{1,12},{2,13},{3,14},{4,15},{5,0},{6,1},{7,2},{8,3},{9,4},{... | collective-permute-start | bytes 331784 | tf_op jit(solution)/shard_map/ppermute | solution.py:37
  227.8 83.2 %collective-permute-start.11 = (bf16[1,1,55296]{2,0,1:T(2,128)(2,1)}, bf16[1,1,55296]{2,0,1:T(2,128)(2,1)}, u32[]{:S(2)}, u32[]{:S(2)}) collective-permute-start(bf16[1,1,55296]{2,0,1:T(2,128)(2,1)} %get-tuple-element.23), channel_id=1, source_target_pairs={{0,12},{1,13},{2,14},{3,15},{4,0},{5,1},{6,2},{7,3},{8,4},{9,5},{1... | collective-permute-start | bytes 331784 | tf_op jit(solution)/shard_map/ppermute | solution.py:37
  230.5 85.7 %collective-permute-start.12 = (bf16[1,1,55296]{2,0,1:T(2,128)(2,1)}, bf16[1,1,55296]{2,0,1:T(2,128)(2,1)}, u32[]{:S(2)}, u32[]{:S(2)}) collective-permute-start(bf16[1,1,55296]{2,0,1:T(2,128)(2,1)} %get-tuple-element.22), channel_id=1, source_target_pairs={{0,13},{1,14},{2,15},{3,0},{4,1},{5,2},{6,3},{7,4},{8,5},{9,6},{10... | collective-permute-start | bytes 331784 | tf_op jit(solution)/shard_map/ppermute | solution.py:37
  236.6 84.7 %collective-permute-start.13 = (bf16[1,1,55296]{2,0,1:T(2,128)(2,1)}, bf16[1,1,55296]{2,0,1:T(2,128)(2,1)}, u32[]{:S(2)}, u32[]{:S(2)}) collective-permute-start(bf16[1,1,55296]{2,0,1:T(2,128)(2,1)} %get-tuple-element.21), channel_id=1, source_target_pairs={{0,14},{1,15},{2,0},{3,1},{4,2},{5,3},{6,4},{7,5},{8,6},{9,7},{10,... | collective-permute-start | bytes 331784 | tf_op jit(solution)/shard_map/ppermute | solution.py:37
  236.6 89.8 %collective-permute-start.14 = (bf16[1,1,55296]{2,0,1:T(2,128)(2,1)}, bf16[1,1,55296]{2,0,1:T(2,128)(2,1)}, u32[]{:S(2)}, u32[]{:S(2)}) collective-permute-start(bf16[1,1,55296]{2,0,1:T(2,128)(2,1)} %get-tuple-element.20), channel_id=1, source_target_pairs={{0,15},{1,0},{2,1},{3,2},{4,3},{5,4},{6,5},{7,6},{8,7},{9,8},{10,9... | collective-permute-start | bytes 331784 | tf_op jit(solution)/shard_map/ppermute | solution.py:37
  239.3 366.3 %reduce-scatter.2.cloned.1.call-start = ((), (), s32[]{:S(2)}) async-start(), calls=%async_computation.6 | async-start | bytes 4718592 | tf_op jit(solution)/shard_map/reduce_scatter | solution.py:91
  436.8 67.9 %all-to-all-start.3 = ((bf16[16,1,72]{2,1,0:T(2,128)(2,1)}), bf16[16,1,72]{2,1,0:T(2,128)(2,1)S(1)}, u32[]{:S(2)}, u32[]{:S(2)}) async-start(bf16[16,1,72]{2,1,0:T(2,128)(2,1)} %convert_element_type.105), calls=%async_computation.3 | async-start | bytes 16384 | tf_op jit(solution)/shard_map/all_to_all | solution.py:104
  504.7 47.4 %all-to-all-start.2 = ((bf16[16,2,27648]{2,1,0:T(2,128)(2,1)}), bf16[16,2,27648]{2,1,0:T(2,128)(2,1)S(1)}, u32[]{:S(2)}, u32[]{:S(2)}) async-start(bf16[16,2,27648]{2,1,0:T(2,128)(2,1)} %reshape.291), calls=%async_computation.2 | async-start | bytes 3538944 | tf_op jit(solution)/shard_map/all_to_all | solution.py:103
  (6 other events, 33.3 us)
Sparse Core Ops, SparseCore 0:
  239.4 61.8 all-gather.1
  421.6 60.4 reduce-scatter.1
